TPU v7x, 32 devices: a whole 2x2x4 slice. The times are simulated.
32 devices in a mesh: groups: 2 (over x), ctx: 16 (over z, y, core).
Axes of the slice: x: 2, y: 2, z: 4, core: 2. Of those that a mesh axis runs over, the one named last changes fastest.
Arguments:
- queries: bfloat16 [4096, 4096], P(('groups', 'ctx')), parts along dimension 0, may hold values from -5 to 5
- keys: bfloat16 [3, 4096, 1024], P(None, ('groups', 'ctx')), parts along dimension 1, may hold values from -5 to 5
- values: bfloat16 [3, 4096, 1024], P(None, ('groups', 'ctx')), parts along dimension 1, may hold values from -5 to 5
- picks: int32 [32, 8, 2], P(('groups', 'ctx')), parts along dimension 0, may hold values from 1 to 15, as said below
Outputs:
- attended: bfloat16 [4096, 4096], P(('groups', 'ctx')), parts along dimension 0
There are 2 independent parts, one for each index of `groups`. A program takes and returns all parts, laid end to end along the dimension named above; each array names one. Nothing has to cross between parts.
Inputs may be any that keep to these rules, and one draw needn't show every extreme that they name: `picks`: each entry is a block before the query's own block and never block 0. Rows 2q and 2q + 1 are equal (one query block). The 2 entries of one head differ in (entry mod 8); within a row no value of (entry mod 8) occurs more than 2 times, and one occurs exactly 2 times.
All inputs are finite; a program needn't handle non-finite values.
Results may differ from a plain program's by a relative error of at most 0.0048.
Values may be sent and summed in bfloat16 or wider, within the bound.
A program may use at most 64 MiB of HBM per device.

v0:
```python
import jax
import jax.numpy as jnp
from jax import lax
from jax.sharding import PartitionSpec as P

BLK = 256
HD = 128
KVH = 8
QH = 32
GRP = 4
FURTHER = 2


def from_root(block, axis, source):
    block = jnp.where(lax.axis_index(axis) == source, block, jnp.zeros_like(block))
    return lax.psum(block, axis)


def shifted(block, axis, distance):
    devices = range(lax.axis_size(axis))
    route = [(i - distance, i) for i in devices if i - distance in devices]
    return lax.ppermute(block, axis, route)


def attend(query_rows, key_cat, value_cat, usable):
    half_rows = query_rows.shape[0]
    score_scale = HD ** (-0.5)
    grouped = query_rows.reshape(half_rows, KVH, GRP, HD)
    results = []
    for kv_head in range(KVH):
        scores = (
            jnp.einsum(
                "tgd,kd->gtk",
                grouped[:, kv_head],
                key_cat[kv_head],
                preferred_element_type=jnp.float32,
            )
            * score_scale
        )
        scores = jnp.where(usable[None], scores, -jnp.inf)
        highest = jnp.max(scores, axis=-1, keepdims=True)
        weights = jnp.exp(scores - highest)
        totals = jnp.sum(weights, axis=-1)
        rounded = weights.astype(jnp.bfloat16)
        blended = jnp.einsum(
            "gtk,kd->tgd", rounded, value_cat[kv_head], preferred_element_type=jnp.float32
        )
        results.append(blended / totals.T[:, :, None])
    return jnp.stack(results, axis=1).reshape(half_rows, QH * HD).astype(jnp.bfloat16)


def key_mask(odd_half, half_rows):
    picked_end = (1 + FURTHER) * BLK
    own_start = picked_end + half_rows
    columns = jnp.arange(own_start + half_rows)[None, :]
    query_pos = jnp.arange(half_rows)[:, None]
    before = columns < picked_end
    earlier = (columns >= picked_end) & (columns < own_start) & odd_half
    causal = (columns >= own_start) & (columns - own_start <= query_pos)
    return before | earlier | causal


def rank_among(pair_table):
    lead_shape = pair_table.shape[:-2]
    entry_count = KVH * FURTHER
    flat = pair_table.reshape(lead_shape + (entry_count,))
    entry_ids = jnp.arange(entry_count)
    lower = entry_ids[None, :] < entry_ids[:, None]
    same = flat[..., :, None] == flat[..., None, :]
    ranks = jnp.sum((same & lower).astype(jnp.int32), axis=-1)
    return ranks.reshape(pair_table.shape)


def shards(queries, keys, values, picks):
    ctx_count = lax.axis_size("ctx")
    my_index = lax.axis_index("ctx")
    pair_count = ctx_count // 2
    slot_count = (FURTHER * KVH + pair_count - 1) // pair_count
    row_count, half_rows, width = keys.shape
    key_heads = keys.reshape(row_count, half_rows, KVH, HD)
    value_heads = values.reshape(row_count, half_rows, KVH, HD)
    request = lax.all_gather(picks, "ctx", axis=0, tiled=True)
    pair_wanted = request % pair_count
    row_wanted = request // pair_count
    rank_wanted = rank_among(pair_wanted)
    served = pair_wanted == my_index // 2
    row_ids = jnp.arange(row_count, dtype=jnp.int32)
    slot_ids = jnp.arange(slot_count, dtype=jnp.int32)
    own_pairs = picks[0] % pair_count
    own_ranks = rank_among(own_pairs)
    sources = jnp.stack([2 * own_pairs, 2 * own_pairs + 1], axis=-1)
    hit_table = (
        served[..., None, None]
        & (rank_wanted[..., None, None] == slot_ids[:, None])
        & (row_wanted[..., None, None] == row_ids)
    )
    hit_table = hit_table.astype(jnp.int32).sum(axis=2).astype(jnp.bfloat16)
    send_keys = jnp.einsum(
        "nhmr,rthd->nmtd", hit_table, key_heads, preferred_element_type=jnp.float32
    ).astype(jnp.bfloat16)
    send_values = jnp.einsum(
        "nhmr,rthd->nmtd", hit_table, value_heads, preferred_element_type=jnp.float32
    ).astype(jnp.bfloat16)
    send_keys, send_values = (send_keys, send_values)
    got_keys, got_values = (
        lax.all_to_all(send_keys, "ctx", split_axis=0, concat_axis=0, tiled=True),
        lax.all_to_all(send_values, "ctx", split_axis=0, concat_axis=0, tiled=True),
    )
    picked_keys = got_keys[sources, own_ranks[..., None]]
    picked_values = got_values[sources, own_ranks[..., None]]
    picked_keys = picked_keys.reshape(KVH, FURTHER * 2 * half_rows, HD)
    picked_values = picked_values.reshape(KVH, FURTHER * 2 * half_rows, HD)
    leading_keys = []
    leading_values = []
    for root_index in (0, 1):
        head_key, head_value = (
            from_root(keys[0], "ctx", root_index),
            from_root(values[0], "ctx", root_index),
        )
        leading_keys.append(head_key)
        leading_values.append(head_value)

    def per_head(block_rows):
        return block_rows.reshape(-1, KVH, HD).transpose(1, 0, 2)

    own_keys = keys[row_count - 1]
    own_values = values[row_count - 1]
    earlier_keys, earlier_values = shifted((own_keys, own_values), "ctx", 1)
    key_cat = jnp.concatenate(
        [
            per_head(jnp.concatenate(leading_keys, axis=0)),
            picked_keys,
            per_head(earlier_keys),
            per_head(own_keys),
        ],
        axis=1,
    )
    value_cat = jnp.concatenate(
        [
            per_head(jnp.concatenate(leading_values, axis=0)),
            picked_values,
            per_head(earlier_values),
            per_head(own_values),
        ],
        axis=1,
    )
    usable = key_mask(my_index % 2 == 1, half_rows)
    return attend(queries, key_cat, value_cat, usable)


def solution(mesh):
    placed = (
        P(("groups", "ctx"), None),
        P(None, ("groups", "ctx"), None),
        P(None, ("groups", "ctx"), None),
        P(("groups", "ctx"), None, None),
    )
    return jax.shard_map(
        shards, mesh=mesh, in_specs=placed, out_specs=P(("groups", "ctx"), None), check_vma=False
    )
```

profile of v0, /device:TPU:25, one launch (start us, length us, event | category | flops | bytes accessed | tf_op | source)
XLA Modules:
  0.0 198.7 jit_solution(15062475570701220847)
XLA Ops:
  6.5 1.1 fusion.89
  7.7 0.8 copy.201
  8.5 3.7 %collective-permute-start.1 = (bf16[128,1024]{0,1:T(8,128)(2,1)}, bf16[128,1024]{0,1:T(8,128)(2,1)}, u32[]{:S(2)}, u32[]{:S(2)}) collective-permute-start(bf16[128,1024]{0,1:T(8,128)(2,1)} %bitcast.31), channel_id=1, source_target_pairs={{0,1},{1,2},{2,3},{3,4},{4,5},{5,6},{6,7},{7,8},{8,9},{9,10},{10,1... | collective-permute-start | bytes 786440 | tf_op jit(solution)/shard_map/ppermute | solution.py:22
  12.3 15.8 %all_gather.3 = s32[16,8,2]{1,2,0:T(2,128)S(1)} all-gather(s32[1,8,2]{1,2,0:T(2,128)} %param.7), channel_id=1, replica_groups=mesh['groups'=2,'ctx'=16] {'ctx'}, dimensions={0}, use_global_device_ids=true | all-gather | bytes 1088 | tf_op jit(solution)/shard_map/all_gather | solution.py:82
  29.5 1.3 copy.166
  30.7 8.4 %all-to-all-start.1 = ((bf16[16,2,128,128]{3,2,1,0:T(8,128)(2,1)}), bf16[16,2,128,128]{3,2,1,0:T(8,128)(2,1)S(1)}, u32[]{:S(2)}, u32[]{:S(2)}) async-start(bf16[16,2,128,128]{3,2,1,0:T(8,128)(2,1)} %copy.166), calls=%async_computation.1 | async-start | bytes 2097152 | tf_op jit(solution)/shard_map/all_to_all | solution.py:106
  39.2 0.8 slice_bitcast_fusion.48
  40.0 3.5 %collective-permute-start = (bf16[128,1024]{1,0:T(8,128)(2,1)}, bf16[128,1024]{1,0:T(8,128)(2,1)}, u32[]{:S(2)}, u32[]{:S(2)}) collective-permute-start(bf16[128,1024]{1,0:T(8,128)(2,1)} %get-tuple-element.13), channel_id=1, source_target_pairs={{0,1},{1,2},{2,3},{3,4},{4,5},{5,6},{6,7},{7,8},{8,9},{9,10},{10,1... | collective-permute-start | bytes 786440 | tf_op jit(solution)/shard_map/ppermute | solution.py:22
  43.8 1.0 select_bitcast_fusion.1
  46.2 1.3 copy.170
  47.5 1.8 copy.169
  49.6 1.3 copy.156
  50.9 0.9 fusion.69
  51.8 1.8 copy.168
  53.6 1.8 copy.160
  55.4 85.9 %all-reduce.3.cloned.1.call-done = (bf16[128,1024]{0,1:T(8,128)(2,1)}, bf16[128,1024]{0,1:T(8,128)(2,1)}, bf16[128,1024]{0,1:T(8,128)(2,1)}, bf16[128,1024]{0,1:T(8,128)(2,1)}) async-done(((bf16[128,1024]{0,1:T(8,128)(2,1)}, bf16[128,1024]{0,1:T(8,128)(2,1)}, bf16[128,1024]{0,1:T(8,128)(2,1)}, bf16[128,1024]{0,1:T(8,128)(2,1)}), (bf16[128,1024]{0,1:T(8,128)(2,1)}, bf16[128,1024]{0,1:T(8,128)(2,1)}, ...) | async-done | bytes 1048592 | tf_op jit(solution)/shard_map/psum | solution.py:16
  141.3 1.1 pad_maximum_fusion.3
  142.4 1.0 copy.164
  143.5 0.9 pad_maximum_fusion.2
  144.3 7.3 %all-to-all-start = ((bf16[16,2,128,128]{3,2,1,0:T(8,128)(2,1)}), bf16[16,2,128,128]{3,2,1,0:T(8,128)(2,1)S(1)}, u32[]{:S(2)}, u32[]{:S(2)}) async-start(bf16[16,2,128,128]{3,2,1,0:T(8,128)(2,1)} %copy.156), calls=%async_computation | async-start | bytes 2097152 | tf_op jit(solution)/shard_map/all_to_all | solution.py:107
  151.6 0.7 gather_fusion.1
  152.4 1.4 pad_maximum_fusion.1
  153.9 2.3 %fusion.90 = (f32[4,128]{1,0:T(4,128)}, f32[4,128,1024]{1,2,0:T(8,128)}) fusion(bf16[128,8,4,128]{0,3,2,1:T(8,128)(2,1)S(1)} %bitcast.356, bf16[8,1024,128]{2,1,0:T(8,128)(2,1)S(1)} %pad_maximum_fusion.1, pred[128,1024]{0,1:T(8,128)(4,1)S(1)} %fusion.69), kind=kOutput, calls=%fused_computation.170 | convolution fusion | flops 135790080 | bytes 2623488 | tf_op jit(solution)/shard_map/tgd,kd->gtk/dot_general | solution.py:32
  156.2 2.3 %fusion.91 = (f32[4,128]{1,0:T(4,128)}, f32[4,128,1024]{1,2,0:T(8,128)}) fusion(bf16[128,8,4,128]{0,3,2,1:T(8,128)(2,1)S(1)} %bitcast.357, bf16[8,1024,128]{2,1,0:T(8,128)(2,1)S(1)} %pad_maximum_fusion.1, pred[128,1024]{0,1:T(8,128)(4,1)S(1)} %fusion.69), kind=kOutput, calls=%fused_computation.171 | convolution fusion | flops 135790080 | bytes 2623488 | tf_op jit(solution)/shard_map/tgd,kd->gtk/dot_general | solution.py:32
  158.5 2.3 %fusion.92 = (f32[4,128]{1,0:T(4,128)}, f32[4,128,1024]{1,2,0:T(8,128)}) fusion(bf16[128,8,4,128]{0,3,2,1:T(8,128)(2,1)S(1)} %bitcast.358, bf16[8,1024,128]{2,1,0:T(8,128)(2,1)S(1)} %pad_maximum_fusion.1, pred[128,1024]{0,1:T(8,128)(4,1)S(1)} %fusion.69), kind=kOutput, calls=%fused_computation.172 | convolution fusion | flops 135790080 | bytes 2623488 | tf_op jit(solution)/shard_map/tgd,kd->gtk/dot_general | solution.py:32
  160.9 2.3 %fusion.93 = (f32[4,128]{1,0:T(4,128)}, f32[4,128,1024]{1,2,0:T(8,128)}) fusion(bf16[128,8,4,128]{0,3,2,1:T(8,128)(2,1)S(1)} %bitcast.359, bf16[8,1024,128]{2,1,0:T(8,128)(2,1)S(1)} %pad_maximum_fusion.1, pred[128,1024]{0,1:T(8,128)(4,1)S(1)} %fusion.69), kind=kOutput, calls=%fused_computation.173 | convolution fusion | flops 135790080 | bytes 2623488 | tf_op jit(solution)/shard_map/tgd,kd->gtk/dot_general | solution.py:32
  163.2 2.4 %fusion.94 = (f32[4,128]{1,0:T(4,128)}, f32[4,128,1024]{1,2,0:T(8,128)}) fusion(bf16[128,8,4,128]{0,3,2,1:T(8,128)(2,1)S(1)} %bitcast.360, bf16[8,1024,128]{2,1,0:T(8,128)(2,1)S(1)} %pad_maximum_fusion.1, pred[128,1024]{0,1:T(8,128)(4,1)S(1)} %fusion.69), kind=kOutput, calls=%fused_computation.174 | convolution fusion | flops 135790080 | bytes 2623488 | tf_op jit(solution)/shard_map/tgd,kd->gtk/dot_general | solution.py:32
  165.6 1.7 fusion.95
  167.3 1.8 fusion.96
  169.1 1.7 fusion.97
  170.8 3.8 %all-to-all-done = bf16[16,2,128,128]{3,2,1,0:T(8,128)(2,1)S(1)} async-done(((bf16[16,2,128,128]{3,2,1,0:T(8,128)(2,1)}), bf16[16,2,128,128]{3,2,1,0:T(8,128)(2,1)S(1)}, u32[]{:S(2)}, u32[]{:S(2)}) %all-to-all-start) | async-done | bytes 1048608 | tf_op jit(solution)/shard_map/all_to_all | solution.py:107
  174.6 0.8 gather_fusion
  175.4 0.5 copy.162
  176.0 1.9 fusion
  178.2 1.3 copy-done.9
  180.5 0.5 fusion.35
  181.0 0.8 copy-done.7
  182.6 0.8 copy-done.6
  183.7 0.5 fusion.39
  184.2 0.8 copy-done.5
  185.2 0.5 fusion.41
  185.8 0.8 copy-done.4
  186.8 0.5 fusion.43
  187.4 0.8 copy-done.3
  188.4 0.5 fusion.45
  189.0 0.8 copy-done.2
  190.0 0.5 fusion.47
  190.6 1.3 copy.187
  (85 shorter events, 7.1 us)
Async XLA Ops:
  6.5 22.2 %copy-start = (bf16[3,128,1024]{2,1,0:T(8,128)(2,1)S(1)}, bf16[3,128,1024]{2,1,0:T(8,128)(2,1)}, u32[]{:S(2)}) copy-start(bf16[3,128,1024]{2,1,0:T(8,128)(2,1)} %param.5) | copy-start | bytes 2359300
  8.5 43.3 %collective-permute-start.1 = (bf16[128,1024]{0,1:T(8,128)(2,1)}, bf16[128,1024]{0,1:T(8,128)(2,1)}, u32[]{:S(2)}, u32[]{:S(2)}) collective-permute-start(bf16[128,1024]{0,1:T(8,128)(2,1)} %bitcast.31), channel_id=1, source_target_pairs={{0,1},{1,2},{2,3},{3,4},{4,5},{5,6},{6,7},{7,8},{8,9},{9,10},{10,1... | collective-permute-start | bytes 786440 | tf_op jit(solution)/shard_map/ppermute | solution.py:22
  29.5 9.7 %copy-start.1 = (bf16[3,128,1024]{2,1,0:T(8,128)(2,1)S(1)}, bf16[3,128,1024]{2,1,0:T(8,128)(2,1)}, u32[]{:S(2)}) copy-start(bf16[3,128,1024]{2,1,0:T(8,128)(2,1)} %param.6) | copy-start | bytes 2359300
  30.7 113.6 %all-to-all-start.1 = ((bf16[16,2,128,128]{3,2,1,0:T(8,128)(2,1)}), bf16[16,2,128,128]{3,2,1,0:T(8,128)(2,1)S(1)}, u32[]{:S(2)}, u32[]{:S(2)}) async-start(bf16[16,2,128,128]{3,2,1,0:T(8,128)(2,1)} %copy.166), calls=%async_computation.1 | async-start | bytes 2097152 | tf_op jit(solution)/shard_map/all_to_all | solution.py:106
  39.1 102.1 %all-reduce.3.cloned.1.call-start = ((), (), s32[]{:S(2)}) async-start(), calls=%async_computation.2 | async-start | bytes 2097152 | tf_op jit(solution)/shard_map/psum | solution.py:16
  40.0 4.9 %copy-start.16 = (s32[1,8,2]{1,2,0:T(2,128)S(1)}, s32[1,8,2]{1,2,0:T(2,128)}, u32[]{:S(2)}) copy-start(s32[1,8,2]{1,2,0:T(2,128)} %param.7) | copy-start | bytes 196
  40.0 13.6 %collective-permute-start = (bf16[128,1024]{1,0:T(8,128)(2,1)}, bf16[128,1024]{1,0:T(8,128)(2,1)}, u32[]{:S(2)}, u32[]{:S(2)}) collective-permute-start(bf16[128,1024]{1,0:T(8,128)(2,1)} %get-tuple-element.13), channel_id=1, source_target_pairs={{0,1},{1,2},{2,3},{3,4},{4,5},{5,6},{6,7},{7,8},{8,9},{9,10},{10,1... | collective-permute-start | bytes 786440 | tf_op jit(solution)/shard_map/ppermute | solution.py:22
  44.8 1.3 copy-start.12
  141.3 2.2 %copy-start.14 = (bf16[128,1024]{0,1:T(8,128)(2,1)S(1)}, bf16[128,1024]{0,1:T(8,128)(2,1)}, u32[]{:S(2)}) copy-start(bf16[128,1024]{0,1:T(8,128)(2,1)} %get-tuple-element.7) | copy-start | bytes 786436
  141.3 2.2 %copy-start.15 = (bf16[128,1024]{0,1:T(8,128)(2,1)S(1)}, bf16[128,1024]{0,1:T(8,128)(2,1)}, u32[]{:S(2)}) copy-start(bf16[128,1024]{0,1:T(8,128)(2,1)} %get-tuple-element.8) | copy-start | bytes 786436
  144.3 30.3 %all-to-all-start = ((bf16[16,2,128,128]{3,2,1,0:T(8,128)(2,1)}), bf16[16,2,128,128]{3,2,1,0:T(8,128)(2,1)S(1)}, u32[]{:S(2)}, u32[]{:S(2)}) async-start(bf16[16,2,128,128]{3,2,1,0:T(8,128)(2,1)} %copy.156), calls=%async_computation | async-start | bytes 2097152 | tf_op jit(solution)/shard_map/all_to_all | solution.py:107
  152.3 1.5 copy-start.13
  170.8 5.1 %copy-start.21 = (f32[4,128]{1,0:T(4,128)S(1)}, f32[4,128]{1,0:T(4,128)}, u32[]{:S(2)}) copy-start(f32[4,128]{1,0:T(4,128)} %get-tuple-element.22) | copy-start | bytes 6148
  175.4 2.5 %copy-start.10 = (bf16[256,1024]{0,1:T(8,128)(2,1)S(1)}, bf16[256,1024]{0,1:T(8,128)(2,1)}, u32[]{:S(2)}) copy-start(bf16[256,1024]{0,1:T(8,128)(2,1)} %pad_maximum_fusion.2) | copy-start | bytes 1572868
  175.4 2.5 %copy-start.11 = (bf16[128,1024]{0,1:T(8,128)(2,1)S(1)}, bf16[128,1024]{0,1:T(8,128)(2,1)}, u32[]{:S(2)}) copy-start(bf16[128,1024]{0,1:T(8,128)(2,1)} %copy.160) | copy-start | bytes 786436
  177.9 1.6 copy-start.9
  178.2 2.0 copy-start.8
  178.2 2.0 copy-start.20
  180.2 1.6 copy-start.7
  180.2 1.6 copy-start.19
  181.8 1.6 copy-start.6
  181.8 1.6 copy-start.18
  183.4 1.6 copy-start.5
  183.4 1.6 copy-start.17
  185.0 1.6 copy-start.4
  186.5 1.6 copy-start.3
  188.1 1.6 copy-start.2
Sparse Core Ops, SparseCore 0:
  45.0 96.2 all-reduce.2
where the time goes:
time: 202 us; the launch traced here: 199 us
  waiting for transfers between devices  89.7 us (44%)
  local copies, waits for them, and re-layouts  24.2 us (12%)
  starting transfers between devices  22.9 us (11%)
  matrix products  22.1 us (11%)
  blocking collectives  15.8 us (8%)
  between operations  13.8 us (7%)
  other arithmetic  10.3 us (5%)
    psum x1, waiting for transfers between devices, from_root(): return lax.psum(block, axis)  85.9 us
    dot_general x8, matrix products, attend(): jnp.einsum('tgd,kd->gtk', grouped[:, kv_head], key_cat[kv_head], preferre...  16.9 us
    all_gather x1, blocking collectives, shards(): request = lax.all_gather(picks, 'ctx', axis=0, tiled=True)  15.8 us
    unnamed x51, local copies, waits for them, and re-layouts  9.14 us
    all_to_all x1, starting transfers between devices, shards(): lax.all_to_all(send_keys, 'ctx', split_axis=0, concat_axis=0, tiled=True)  8.41 us
    all_to_all x1, starting transfers between devices, shards(): lax.all_to_all(send_values, 'ctx', split_axis=0, concat_axis=0, tiled=True)  7.25 us
    ppermute x2, starting transfers between devices, shifted(): return lax.ppermute(block, axis, route)  7.17 us
    dot_general x8, matrix products, attend(): jnp.einsum('gtk,kd->tgd', rounded, value_cat[kv_head], preferred_element_...  4.15 us
  transfers between devices with their start and end apart: 5, of which 2 were waited for; matrix products, arithmetic and copies ran while one was open for 19% of the time, Pallas kernels for 0%

commit v1 on v0

v1 whole, which is shorter than its diff:
```python
import functools
import math

import jax
import jax.numpy as jnp
from jax import lax
from jax.experimental import pallas as pl
from jax.experimental.pallas import tpu as pltpu
from jax.sharding import PartitionSpec as P

HD = 128
KVH = 8
GRP = 4
FURTHER = 2
WANTED = KVH * FURTHER
CHUNKS = 4
MESH = pl.DeviceIdType.MESH
SCALE = HD ** -0.5
EXP2_SCALE = SCALE * math.log2(math.e)


def xor_of(a, b, n):
    a, b = jnp.int32(a), jnp.int32(b)
    total = 0
    bit = 1
    while bit < n:
        total = total + lax.rem(lax.rem(lax.div(a, bit), 2) + lax.rem(lax.div(b, bit), 2), 2) * bit
        bit *= 2
    return total


def partial_attend(rows, keys, values, usable=None):
    scores = lax.dot_general(
        rows, keys, (((1,), (1,)), ((), ())), preferred_element_type=jnp.float32
    )
    if usable is not None:
        scores = jnp.where(usable, scores, -jnp.inf)
    highest = jnp.max(scores, axis=-1, keepdims=True)
    weights = jnp.exp2((scores - highest) * EXP2_SCALE)
    total = jnp.sum(weights, axis=-1, keepdims=True)
    blended = jnp.dot(
        weights.astype(jnp.bfloat16), values, preferred_element_type=jnp.float32
    )
    return blended, highest, total


def kernel(
    n, slots, picks_ref, q_hbm, k_hbm, v_hbm, o_hbm,
    qv, kv, vv, blk, earl, pk, pk_sm, send, recv,
    acc_l, max_l, tot_l, acc_p, max_p, tot_p, stage,
    load_sem, q_sem, root_sem, earl_loc, earl_s, earl_r, pk_s, pk_r, sm_sem,
    blk_s, blk_r, a2a_s, a2a_r, fwd_s, fwd_r, out_sem,
):
    me = lax.axis_index("ctx")
    chip, core = me // 2, me % 2
    z, y = chip // 2, chip % 2
    depth = n // 2
    half = q_hbm.shape[0]
    last = k_hbm.shape[0] - 1
    sibling = chip * 2 + 1 - core

    def peer(k):
        return xor_of(chip, k, n) * 2 + core

    def remote(src, dst, s_sem, r_sem, dest):
        return pltpu.make_async_remote_copy(
            src_ref=src, dst_ref=dst, send_sem=s_sem, recv_sem=r_sem,
            device_id={"ctx": dest}, device_id_type=MESH,
        )

    def cache_loads(head):
        window = pl.ds(pl.multiple_of(head * HD, HD), HD)
        return [
            pltpu.make_async_copy(src.at[row, :, window], dst.at[row * KVH + head], load_sem.at[i, row, head])
            for i, (src, dst) in enumerate(((k_hbm, kv), (v_hbm, vv)))
            for row in range(last + 1)
        ]

    def query_load(head, g):
        window = pl.ds(pl.multiple_of((head * GRP + g) * HD, HD), HD)
        return pltpu.make_async_copy(q_hbm.at[:, window], qv.at[head, pl.ds(g * half, half)], q_sem.at[head, g])

    root_loads = [
        pltpu.make_async_copy(src.at[0], blk.at[core, i], root_sem.at[i])
        for i, src in enumerate((k_hbm, v_hbm))
    ]

    @pl.when(chip == 0)
    def _():
        for copy in root_loads:
            copy.start()

    def load_cache(head, carry):
        for copy in cache_loads(head):
            copy.start()
        return carry

    lax.fori_loop(0, KVH, load_cache, 0)

    barrier = pltpu.get_barrier_semaphore()

    def greet(k, carry):
        pl.semaphore_signal(barrier, inc=1, device_id={"ctx": peer(k)}, device_id_type=MESH)
        return carry

    lax.fori_loop(1, n, greet, 0)
    pl.semaphore_signal(barrier, inc=1, device_id={"ctx": sibling}, device_id_type=MESH)

    lanes = lax.broadcasted_iota(jnp.int32, (KVH, HD), 1)
    subs = lax.broadcasted_iota(jnp.int32, (KVH, HD), 0)
    mine = picks_ref[0]
    spread = jnp.where(lanes == subs, mine[:, 0:1], 0)
    spread = spread + jnp.where(lanes == subs + KVH, mine[:, 1:2], 0)
    pk[0] = jnp.sum(spread, axis=0, keepdims=True)

    pl.semaphore_wait(barrier, n)

    def pk_copy(k):
        return remote(pk.at[0], pk.at[k], pk_s.at[k], pk_r.at[k], peer(k))

    def pk_send(k, carry):
        pk_copy(k).start()
        return carry

    lax.fori_loop(1, n, pk_send, 0)

    rows_of = half // (CHUNKS // 2)

    def blk_part(side, ch):
        return blk.at[side, ch // (CHUNKS // 2), pl.ds((ch % (CHUNKS // 2)) * rows_of, rows_of)]

    column = y == core
    routes = [
        (column & (z == 0), (2 + y) * 2 + core),
        (column & (z >= 2) & (z + 1 < depth), ((z + 1) * 2 + y) * 2 + core),
        (column & jnp.logical_not((core == 1) & (z == 0)), (z * 2 + 1 - y) * 2 + core),
        ((chip == 0) & (core == 1), 3),
    ]
    if depth > 2:
        routes.append((column & (z == 0), (4 + y) * 2 + core))

    def blk_copy(kind, ch):
        return remote(
            blk_part(core, ch), blk_part(core, ch), blk_s.at[kind, ch], blk_r.at[0, ch], routes[kind][1]
        )

    def blk_sib(ch):
        return remote(
            blk_part(core, ch), blk_part(core, ch), blk_s.at[len(routes), ch], blk_r.at[1, ch], sibling
        )

    def blk_start(ch):
        for kind, (wanted, _) in enumerate(routes):
            @pl.when(wanted)
            def _():
                blk_copy(kind, ch).start()
        blk_sib(ch).start()

    @pl.when(chip == 0)
    def _():
        for copy in root_loads:
            copy.wait()
        for ch in range(CHUNKS):
            blk_start(ch)

    earl_copies = [
        remote(src.at[last], earl.at[i], earl_s.at[i], earl_r.at[i], sibling)
        for i, src in enumerate((k_hbm, v_hbm))
    ]
    earl_locals = [
        pltpu.make_async_copy(src.at[last], earl.at[i], earl_loc.at[i])
        for i, src in enumerate((k_hbm, v_hbm))
    ]

    @pl.when(core == 0)
    def _():
        for copy in earl_copies + earl_locals:
            copy.start()

    def load_queries(head, carry):
        for g in range(GRP):
            query_load(head, g).start()
        return carry

    lax.fori_loop(0, KVH, load_queries, 0)

    def wait_cache(head, carry):
        for copy in cache_loads(head):
            copy.wait()
        return carry

    lax.fori_loop(0, KVH, wait_cache, 0)

    def pk_wait(k, carry):
        pk_copy(k).wait_recv()
        return carry

    lax.fori_loop(1, n, pk_wait, 0)
    to_scalar = pltpu.make_async_copy(pk, pk_sm, sm_sem)
    to_scalar.start()
    to_scalar.wait()

    def served(k, pair):
        found = [(jnp.int32(0), jnp.int32(0))] * slots
        count = jnp.int32(0)
        for e in range(WANTED):
            block = pk_sm[k, 0, e]
            match = lax.rem(block, n) == pair
            for m in range(slots):
                hit = match & (count == m)
                head, row = found[m]
                found[m] = (jnp.where(hit, e % KVH, head), jnp.where(hit, lax.div(block, n), row))
            count = count + match.astype(jnp.int32)
        return found

    def gather(k, dst):
        for m, (head, row) in enumerate(served(k, chip)):
            dst[m, 0] = kv[row * KVH + head]
            dst[m, 1] = vv[row * KVH + head]

    def a2a_copy(k):
        return remote(send.at[k], recv.at[k, core], a2a_s.at[k], a2a_r.at[k], peer(k))

    def a2a_send(i, carry):
        k = n - 1 - i
        gather(k, send.at[k])
        a2a_copy(k).start()
        return carry

    lax.fori_loop(0, n - 1, a2a_send, 0)
    gather(0, recv.at[0, core])

    def fwd_copy(k):
        return remote(recv.at[k, core], recv.at[k, core], fwd_s.at[k], fwd_r.at[k], sibling)

    fwd_copy(0).start()

    @pl.when(chip != 0)
    def _():
        for ch in range(CHUNKS):
            blk_copy(0, ch).wait_recv()
            blk_start(ch)

    def wait_queries(head, carry):
        for g in range(GRP):
            query_load(head, g).wait()
        return carry

    lax.fori_loop(0, KVH, wait_queries, 0)

    @pl.when(core == 0)
    def _():
        for copy in earl_locals:
            copy.wait()

    @pl.when(core == 1)
    def _():
        for copy in earl_copies:
            copy.wait_recv()

    for ch in range(CHUNKS):
        blk_sib(ch).wait_recv()

    def local_head(head, carry):
        window = pl.ds(pl.multiple_of(head * HD, HD), HD)
        keys = jnp.concatenate(
            [blk[0, 0, :, window], blk[1, 0, :, window], earl[0, :, window], kv[last * KVH + head]], axis=0
        )
        values = jnp.concatenate(
            [blk[0, 1, :, window], blk[1, 1, :, window], earl[1, :, window], vv[last * KVH + head]], axis=0
        )
        shape = (GRP * half, 4 * half)
        columns = lax.broadcasted_iota(jnp.int32, shape, 1)
        query_pos = lax.broadcasted_iota(jnp.int32, shape, 0) % half
        usable = columns < 2 * half + half * core
        usable = usable | ((columns >= 3 * half) & (columns - 3 * half <= query_pos))
        blended, highest, total = partial_attend(qv[head], keys, values, usable)
        acc_l[head] = blended
        max_l[head] = highest
        tot_l[head] = total
        return carry

    lax.fori_loop(0, KVH, local_head, 0)

    def picked(k):
        for m, (head, _) in enumerate(served(0, xor_of(chip, k, n))):
            keys = jnp.concatenate([recv[k, 0, m, 0], recv[k, 1, m, 0]], axis=0)
            values = jnp.concatenate([recv[k, 0, m, 1], recv[k, 1, m, 1]], axis=0)
            blended, highest, total = partial_attend(qv[head], keys, values)
            acc_p[k * slots + m] = blended
            max_p[k * slots + m] = highest
            tot_p[k * slots + m] = total

    def forward(k):
        a2a_copy(k).wait_recv()
        fwd_copy(k).start()

    def sib_wait(k):
        remote(
            recv.at[k, 1 - core], recv.at[k, 1 - core], fwd_s.at[k], fwd_r.at[k], sibling
        ).wait_recv()

    def step(i, carry):
        k = (n - i) % n
        forward(n - 1 - i)
        sib_wait(k)
        picked(k)
        return carry

    lax.fori_loop(0, n - 1, step, 0)
    sib_wait(1)
    picked(1)

    def out_copy(head):
        window = pl.ds(pl.multiple_of(head * GRP * HD, GRP * HD), GRP * HD)
        return pltpu.make_async_copy(stage.at[:, window], o_hbm.at[:, window], out_sem.at[head])

    def merge(head, carry):
        parts = [(acc_l[head], max_l[head], tot_l[head])]
        for s in range(FURTHER):
            entry = s * KVH + head
            pair = lax.rem(pk_sm[0, 0, entry], n)
            rank = jnp.int32(0)
            for e in range(WANTED):
                same = (lax.rem(pk_sm[0, 0, e], n) == pair) & (e < entry)
                rank = rank + same.astype(jnp.int32)
            index = xor_of(pair, chip, n) * slots + jnp.minimum(rank, slots - 1)
            parts.append((acc_p[index], max_p[index], tot_p[index]))
        top = functools.reduce(jnp.maximum, [part[1] for part in parts])
        shares = [jnp.exp2((part[1] - top) * EXP2_SCALE) for part in parts]
        total = sum(share * part[2] for share, part in zip(shares, parts))
        result = sum((share / total) * part[0] for share, part in zip(shares, parts))
        result = result.astype(stage.dtype)
        for g in range(GRP):
            window = pl.ds(pl.multiple_of((head * GRP + g) * HD, HD), HD)
            stage[:, window] = result[g * half:(g + 1) * half]
        out_copy(head).start()
        return carry

    lax.fori_loop(0, KVH, merge, 0)

    def drain(k, carry):
        pk_copy(k).wait_send()
        a2a_copy(k).wait_send()
        return carry

    lax.fori_loop(1, n, drain, 0)

    def drain_fwd(k, carry):
        fwd_copy(k).wait_send()
        return carry

    lax.fori_loop(0, n, drain_fwd, 0)
    for ch in range(CHUNKS):
        for kind, (wanted, _) in enumerate(routes):
            @pl.when(wanted)
            def _():
                blk_copy(kind, ch).wait_send()
        blk_sib(ch).wait_send()

    @pl.when(core == 0)
    def _():
        for copy in earl_copies:
            copy.wait_send()

    def drain_out(head, carry):
        out_copy(head).wait()
        return carry

    lax.fori_loop(0, KVH, drain_out, 0)


def solution(mesh):
    n = mesh.shape["ctx"] // 2
    slots = (WANTED + n - 1) // n
    bf16, f32 = jnp.bfloat16, jnp.float32

    def shard(queries, keys, values, picks):
        half, width = queries.shape
        rows = keys.shape[0]
        kv_width = keys.shape[2]
        dma = pltpu.SemaphoreType.DMA
        anywhere = pl.BlockSpec(memory_space=pl.ANY)
        return pl.pallas_call(
            functools.partial(kernel, n, slots),
            out_shape=jax.ShapeDtypeStruct(queries.shape, bf16),
            in_specs=[pl.BlockSpec(memory_space=pltpu.VMEM), anywhere, anywhere, anywhere],
            out_specs=anywhere,
            scratch_shapes=[
                pltpu.VMEM((KVH, GRP * half, HD), bf16),
                pltpu.VMEM((rows * KVH, half, HD), bf16),
                pltpu.VMEM((rows * KVH, half, HD), bf16),
                pltpu.VMEM((2, 2, half, kv_width), bf16),
                pltpu.VMEM((2, half, kv_width), bf16),
                pltpu.VMEM((n, 1, HD), jnp.int32),
                pltpu.SMEM((n, 1, HD), jnp.int32),
                pltpu.VMEM((n, slots, 2, half, HD), bf16),
                pltpu.VMEM((n, 2, slots, 2, half, HD), bf16),
                pltpu.VMEM((KVH, GRP * half, HD), f32),
                pltpu.VMEM((KVH, GRP * half, 1), f32),
                pltpu.VMEM((KVH, GRP * half, 1), f32),
                pltpu.VMEM((n * slots, GRP * half, HD), f32),
                pltpu.VMEM((n * slots, GRP * half, 1), f32),
                pltpu.VMEM((n * slots, GRP * half, 1), f32),
                pltpu.VMEM((half, width), bf16),
                dma((2, rows, KVH)), dma((KVH, GRP)), dma((2,)), dma((2,)), dma((2,)), dma((2,)),
                dma((n,)), dma((n,)), dma,
                dma((6, CHUNKS)), dma((2, CHUNKS)),
                dma((n,)), dma((n,)), dma((n,)), dma((n,)), dma((KVH,)),
            ],
            compiler_params=pltpu.CompilerParams(
                collective_id=0, has_side_effects=True, vmem_limit_bytes=56 * 2**20
            ),
        )(picks, queries, keys, values)

    placed = (
        P(("groups", "ctx"), None),
        P(None, ("groups", "ctx"), None),
        P(None, ("groups", "ctx"), None),
        P(("groups", "ctx"), None, None),
    )
    return jax.shard_map(
        shard, mesh=mesh, in_specs=placed, out_specs=P(("groups", "ctx"), None), check_vma=False
    )
```

time: 202 us -> 66.9 us (0.33); the launches traced: 199 us -> 66.7 us
  waiting for transfers between devices: 89.7 us -> 0 us
  Pallas kernels: 0 us -> 63 us
  starting transfers between devices: 22.9 us -> 0 us
  matrix products: 22.1 us -> 0 us
  local copies, waits for them, and re-layouts: 24.2 us -> 3.63 us
  blocking collectives: 15.8 us -> 0 us
  between operations: 13.8 us -> 0.01 us
  other arithmetic: 10.3 us -> 0 us
    psum x1 -> x0, waiting for transfers between devices: 85.9 us -> none  [from_root(): return lax.psum(block, axis)]
    pallas_call x0 -> x1, Pallas kernels: none -> 63 us  [shard(): pl.pallas_call(functools.partial(kernel, n, slots), out_shape=jax.ShapeDt...]
    dot_general x18 -> x0, matrix products: 22.1 us -> none  [the longest x8 16.9 us: attend(): jnp.einsum('tgd,kd->gtk', grouped[:, kv_head], key_cat[kv_head], preferre...]
    all_gather x1 -> x0, blocking collectives: 15.8 us -> none  [shards(): request = lax.all_gather(picks, 'ctx', axis=0, tiled=True)]
    all_to_all x2 -> x0, starting transfers between devices: 15.7 us -> none  [the longest x1 8.41 us: shards(): lax.all_to_all(send_keys, 'ctx', split_axis=0, concat_axis=0, tiled=True)]
    ppermute x2 -> x0, starting transfers between devices: 7.17 us -> none  [shifted(): return lax.ppermute(block, axis, route)]
    unnamed x51 -> x2, local copies, waits for them, and re-layouts: 9.14 us -> 3.63 us
    reduce_sum x11 -> x0, other arithmetic: 4.59 us -> none  [the longest x8 3.97 us: attend(): totals = jnp.sum(weights, axis=-1)]
  transfers between devices with their start and end apart: 5 -> 0, of which waited for: 2 -> 0; matrix products, arithmetic and copies ran while one was open for 19% -> 0% of each run, Pallas kernels for 0% -> 0%
where the time goes in v1:
time: 66.9 us; the launch traced here: 66.7 us
  Pallas kernels  63 us (94%)
  local copies, waits for them, and re-layouts  3.63 us (5%)
    pallas_call x1, Pallas kernels, shard(): pl.pallas_call(functools.partial(kernel, n, slots), out_shape=jax.ShapeDt...  63 us
    unnamed x2, local copies, waits for them, and re-layouts  3.63 us

profile of v1, /device:TPU:25, one launch (start us, length us, event | category | flops | bytes accessed | tf_op | source)
XLA Modules:
  0.0 66.7 jit_solution(3785737849569869323)
XLA Ops:
  0.0 1.3 %copy.5.picks_ref = s32[1,8,2]{2,1,0:T(8,128)} copy(s32[1,8,2]{1,2,0:T(2,128)} %param.7) | data formatting | bytes 128 | tf_op args[3]
  1.3 63.0 %shard_map.46 = bf16[128,4096]{1,0:T(8,128)(2,1)} custom-call(s32[1,8,2]{2,1,0:T(8,128)} %copy.5.picks_ref, bf16[128,4096]{1,0:T(8,128)(2,1)} %q_hbm.1, bf16[3,128,1024]{2,1,0:T(8,128)(2,1)} %k_hbm.1, bf16[3,128,1024]{2,1,0:T(8,128)(2,1)} %v_hbm.1), custom_call_target="tpu_custom_call" | custom-call | tf_op jit(solution)/shard_map/pallas_call | solution.py:384
  64.4 2.3 %copy.7 = bf16[128,4096]{1,0:T(8,128)(2,1)} copy(bf16[128,4096]{1,0:T(8,128)(2,1)} %shard_map.46) | data formatting | bytes 2097152

commit v2 on v1

--- a/solution.py
+++ b/solution.py
@@ -45,8 +45,8 @@
 
 
 def kernel(
-    n, slots, picks_ref, q_hbm, k_hbm, v_hbm, o_hbm,
-    qv, kv, vv, blk, earl, pk, pk_sm, send, recv,
+    n, slots, picks_hbm, q_hbm, k_hbm, v_hbm, o_hbm,
+    own_picks, qv, kv, vv, blk, earl, pk, pk_sm, send, recv,
     acc_l, max_l, tot_l, acc_p, max_p, tot_p, stage,
     load_sem, q_sem, root_sem, earl_loc, earl_s, earl_r, pk_s, pk_r, sm_sem,
     blk_s, blk_r, a2a_s, a2a_r, fwd_s, fwd_r, out_sem,
@@ -85,6 +85,9 @@
         for i, src in enumerate((k_hbm, v_hbm))
     ]
 
+    picks_load = pltpu.make_async_copy(picks_hbm, own_picks, sm_sem.at[1])
+    picks_load.start()
+
     @pl.when(chip == 0)
     def _():
         for copy in root_loads:
@@ -108,7 +111,8 @@
 
     lanes = lax.broadcasted_iota(jnp.int32, (KVH, HD), 1)
     subs = lax.broadcasted_iota(jnp.int32, (KVH, HD), 0)
-    mine = picks_ref[0]
+    picks_load.wait()
+    mine = own_picks[0]
     spread = jnp.where(lanes == subs, mine[:, 0:1], 0)
     spread = spread + jnp.where(lanes == subs + KVH, mine[:, 1:2], 0)
     pk[0] = jnp.sum(spread, axis=0, keepdims=True)
@@ -131,13 +135,10 @@
 
     column = y == core
     routes = [
-        (column & (z == 0), (2 + y) * 2 + core),
-        (column & (z >= 2) & (z + 1 < depth), ((z + 1) * 2 + y) * 2 + core),
+        (column & (z + 1 < depth), ((z + 1) * 2 + y) * 2 + core),
         (column & jnp.logical_not((core == 1) & (z == 0)), (z * 2 + 1 - y) * 2 + core),
         ((chip == 0) & (core == 1), 3),
     ]
-    if depth > 2:
-        routes.append((column & (z == 0), (4 + y) * 2 + core))
 
     def blk_copy(kind, ch):
         return remote(
@@ -196,7 +197,7 @@
         return carry
 
     lax.fori_loop(1, n, pk_wait, 0)
-    to_scalar = pltpu.make_async_copy(pk, pk_sm, sm_sem)
+    to_scalar = pltpu.make_async_copy(pk, pk_sm, sm_sem.at[0])
     to_scalar.start()
     to_scalar.wait()
 
@@ -227,7 +228,15 @@
         a2a_copy(k).start()
         return carry
 
-    lax.fori_loop(0, n - 1, a2a_send, 0)
+    for ch in range(CHUNKS):
+        @pl.when(column & (chip != 0))
+        def _():
+            blk_copy(0, ch).wait_recv()
+            blk_start(ch)
+
+        a2a_send(ch, 0)
+
+    lax.fori_loop(CHUNKS, n - 1, a2a_send, 0)
     gather(0, recv.at[0, core])
 
     def fwd_copy(k):
@@ -235,7 +244,7 @@
 
     fwd_copy(0).start()
 
-    @pl.when(chip != 0)
+    @pl.when(jnp.logical_not(column) & (chip != 0))
     def _():
         for ch in range(CHUNKS):
             blk_copy(0, ch).wait_recv()
@@ -257,6 +266,27 @@
     def _():
         for copy in earl_copies:
             copy.wait_recv()
+
+    def picked(k):
+        for m, (head, _) in enumerate(served(0, xor_of(chip, k, n))):
+            keys = jnp.concatenate([recv[k, 0, m, 0], recv[k, 1, m, 0]], axis=0)
+            values = jnp.concatenate([recv[k, 0, m, 1], recv[k, 1, m, 1]], axis=0)
+            blended, highest, total = partial_attend(qv[head], keys, values)
+            acc_p[k * slots + m] = blended
+            max_p[k * slots + m] = highest
+            tot_p[k * slots + m] = total
+
+    def forward(k):
+        a2a_copy(k).wait_recv()
+        fwd_copy(k).start()
+
+    def sib_wait(k):
+        remote(
+            recv.at[k, 1 - core], recv.at[k, 1 - core], fwd_s.at[k], fwd_r.at[k], sibling
+        ).wait_recv()
+
+    sib_wait(0)
+    picked(0)
 
     for ch in range(CHUNKS):
         blk_sib(ch).wait_recv()
@@ -282,32 +312,15 @@
 
     lax.fori_loop(0, KVH, local_head, 0)
 
-    def picked(k):
-        for m, (head, _) in enumerate(served(0, xor_of(chip, k, n))):
-            keys = jnp.concatenate([recv[k, 0, m, 0], recv[k, 1, m, 0]], axis=0)
-            values = jnp.concatenate([recv[k, 0, m, 1], recv[k, 1, m, 1]], axis=0)
-            blended, highest, total = partial_attend(qv[head], keys, values)
-            acc_p[k * slots + m] = blended
-            max_p[k * slots + m] = highest
-            tot_p[k * slots + m] = total
-
-    def forward(k):
-        a2a_copy(k).wait_recv()
-        fwd_copy(k).start()
-
-    def sib_wait(k):
-        remote(
-            recv.at[k, 1 - core], recv.at[k, 1 - core], fwd_s.at[k], fwd_r.at[k], sibling
-        ).wait_recv()
-
     def step(i, carry):
-        k = (n - i) % n
+        k = n - i
         forward(n - 1 - i)
         sib_wait(k)
         picked(k)
         return carry
 
-    lax.fori_loop(0, n - 1, step, 0)
+    forward(n - 1)
+    lax.fori_loop(1, n - 1, step, 0)
     sib_wait(1)
     picked(1)
 
@@ -384,9 +397,10 @@
         return pl.pallas_call(
             functools.partial(kernel, n, slots),
             out_shape=jax.ShapeDtypeStruct(queries.shape, bf16),
-            in_specs=[pl.BlockSpec(memory_space=pltpu.VMEM), anywhere, anywhere, anywhere],
+            in_specs=[anywhere, anywhere, anywhere, anywhere],
             out_specs=anywhere,
             scratch_shapes=[
+                pltpu.VMEM(picks.shape, jnp.int32),
                 pltpu.VMEM((KVH, GRP * half, HD), bf16),
                 pltpu.VMEM((rows * KVH, half, HD), bf16),
                 pltpu.VMEM((rows * KVH, half, HD), bf16),
@@ -404,7 +418,7 @@
                 pltpu.VMEM((n * slots, GRP * half, 1), f32),
                 pltpu.VMEM((half, width), bf16),
                 dma((2, rows, KVH)), dma((KVH, GRP)), dma((2,)), dma((2,)), dma((2,)), dma((2,)),
-                dma((n,)), dma((n,)), dma,
+                dma((n,)), dma((n,)), dma((2,)),
                 dma((6, CHUNKS)), dma((2, CHUNKS)),
                 dma((n,)), dma((n,)), dma((n,)), dma((n,)), dma((KVH,)),
             ],

time: 66.9 us -> 67.2 us (level)
  no operation moved by 1% of the time
where the time goes in v2:
time: 67.2 us; the launch traced here: 67 us
  Pallas kernels  63.3 us (94%)
  local copies, waits for them, and re-layouts  3.63 us (5%)
    pallas_call x1, Pallas kernels, shard(): pl.pallas_call(functools.partial(kernel, n, slots), out_shape=jax.ShapeDt...  63.3 us
    unnamed x2, local copies, waits for them, and re-layouts  3.63 us

profile of v2, /device:TPU:25, one launch (start us, length us, event | category | flops | bytes accessed | tf_op | source)
XLA Modules:
  0.0 67.0 jit_solution(11683223764072480229)
XLA Ops:
  0.0 1.3 %copy.5.picks_hbm = s32[1,8,2]{2,1,0:T(8,128)} copy(s32[1,8,2]{1,2,0:T(2,128)} %param.7) | data formatting | bytes 128 | tf_op args[3]
  1.3 63.3 %shard_map.46 = bf16[128,4096]{1,0:T(8,128)(2,1)} custom-call(s32[1,8,2]{2,1,0:T(8,128)} %copy.5.picks_hbm, bf16[128,4096]{1,0:T(8,128)(2,1)} %q_hbm.1, bf16[3,128,1024]{2,1,0:T(8,128)(2,1)} %k_hbm.1, bf16[3,128,1024]{2,1,0:T(8,128)(2,1)} %v_hbm.1), custom_call_target="tpu_custom_call" | custom-call | tf_op jit(solution)/shard_map/pallas_call | solution.py:397
  64.7 2.3 %copy.7 = bf16[128,4096]{1,0:T(8,128)(2,1)} copy(bf16[128,4096]{1,0:T(8,128)(2,1)} %shard_map.46) | data formatting | bytes 2097152

commit v3 on v2

--- a/solution.py
+++ b/solution.py
@@ -71,9 +71,8 @@
     def cache_loads(head):
         window = pl.ds(pl.multiple_of(head * HD, HD), HD)
         return [
-            pltpu.make_async_copy(src.at[row, :, window], dst.at[row * KVH + head], load_sem.at[i, row, head])
+            pltpu.make_async_copy(src.at[:, :, window], dst.at[head], load_sem.at[i, head])
             for i, (src, dst) in enumerate(((k_hbm, kv), (v_hbm, vv)))
-            for row in range(last + 1)
         ]
 
     def query_load(head, g):
@@ -183,22 +182,27 @@
             query_load(head, g).start()
         return carry
 
-    lax.fori_loop(0, KVH, load_queries, 0)
-
     def wait_cache(head, carry):
         for copy in cache_loads(head):
             copy.wait()
         return carry
 
-    lax.fori_loop(0, KVH, wait_cache, 0)
-
     def pk_wait(k, carry):
         pk_copy(k).wait_recv()
         return carry
+
+    early = column & (chip != 0) & (z <= 1)
+
+    @pl.when(early)
+    def _():
+        for ch in range(2):
+            blk_copy(0, ch).wait_recv()
+            blk_start(ch)
 
     lax.fori_loop(1, n, pk_wait, 0)
     to_scalar = pltpu.make_async_copy(pk, pk_sm, sm_sem.at[0])
     to_scalar.start()
+    lax.fori_loop(0, KVH, wait_cache, 0)
     to_scalar.wait()
 
     def served(k, pair):
@@ -216,8 +220,8 @@
 
     def gather(k, dst):
         for m, (head, row) in enumerate(served(k, chip)):
-            dst[m, 0] = kv[row * KVH + head]
-            dst[m, 1] = vv[row * KVH + head]
+            dst[m, 0] = kv[head, row]
+            dst[m, 1] = vv[head, row]
 
     def a2a_copy(k):
         return remote(send.at[k], recv.at[k, core], a2a_s.at[k], a2a_r.at[k], peer(k))
@@ -229,7 +233,7 @@
         return carry
 
     for ch in range(CHUNKS):
-        @pl.when(column & (chip != 0))
+        @pl.when(column & (chip != 0) & ((z > 1) | (ch >= 2)))
         def _():
             blk_copy(0, ch).wait_recv()
             blk_start(ch)
@@ -243,6 +247,7 @@
         return remote(recv.at[k, core], recv.at[k, core], fwd_s.at[k], fwd_r.at[k], sibling)
 
     fwd_copy(0).start()
+    lax.fori_loop(0, KVH, load_queries, 0)
 
     @pl.when(jnp.logical_not(column) & (chip != 0))
     def _():
@@ -294,10 +299,10 @@
     def local_head(head, carry):
         window = pl.ds(pl.multiple_of(head * HD, HD), HD)
         keys = jnp.concatenate(
-            [blk[0, 0, :, window], blk[1, 0, :, window], earl[0, :, window], kv[last * KVH + head]], axis=0
+            [blk[0, 0, :, window], blk[1, 0, :, window], earl[0, :, window], kv[head, last]], axis=0
         )
         values = jnp.concatenate(
-            [blk[0, 1, :, window], blk[1, 1, :, window], earl[1, :, window], vv[last * KVH + head]], axis=0
+            [blk[0, 1, :, window], blk[1, 1, :, window], earl[1, :, window], vv[head, last]], axis=0
         )
         shape = (GRP * half, 4 * half)
         columns = lax.broadcasted_iota(jnp.int32, shape, 1)
@@ -402,8 +407,8 @@
             scratch_shapes=[
                 pltpu.VMEM(picks.shape, jnp.int32),
                 pltpu.VMEM((KVH, GRP * half, HD), bf16),
-                pltpu.VMEM((rows * KVH, half, HD), bf16),
-                pltpu.VMEM((rows * KVH, half, HD), bf16),
+                pltpu.VMEM((KVH, rows, half, HD), bf16),
+                pltpu.VMEM((KVH, rows, half, HD), bf16),
                 pltpu.VMEM((2, 2, half, kv_width), bf16),
                 pltpu.VMEM((2, half, kv_width), bf16),
                 pltpu.VMEM((n, 1, HD), jnp.int32),
@@ -417,7 +422,7 @@
                 pltpu.VMEM((n * slots, GRP * half, 1), f32),
                 pltpu.VMEM((n * slots, GRP * half, 1), f32),
                 pltpu.VMEM((half, width), bf16),
-                dma((2, rows, KVH)), dma((KVH, GRP)), dma((2,)), dma((2,)), dma((2,)), dma((2,)),
+                dma((2, KVH)), dma((KVH, GRP)), dma((2,)), dma((2,)), dma((2,)), dma((2,)),
                 dma((n,)), dma((n,)), dma((2,)),
                 dma((6, CHUNKS)), dma((2, CHUNKS)),
                 dma((n,)), dma((n,)), dma((n,)), dma((n,)), dma((KVH,)),

time: 67.2 us -> 66.9 us (level)
  no operation moved by 1% of the time
where the time goes in v3:
time: 66.9 us; the launch traced here: 66.6 us
  Pallas kernels  62.9 us (94%)
  local copies, waits for them, and re-layouts  3.63 us (5%)
    pallas_call x1, Pallas kernels, shard(): pl.pallas_call(functools.partial(kernel, n, slots), out_shape=jax.ShapeDt...  62.9 us
    unnamed x2, local copies, waits for them, and re-layouts  3.63 us

profile of v3, /device:TPU:25, one launch (start us, length us, event | category | flops | bytes accessed | tf_op | source)
XLA Modules:
  0.0 66.6 jit_solution(11096873381193113291)
XLA Ops:
  0.0 1.3 %copy.5.picks_hbm = s32[1,8,2]{2,1,0:T(8,128)} copy(s32[1,8,2]{1,2,0:T(2,128)} %param.7) | data formatting | bytes 128 | tf_op args[3]
  1.3 62.9 %shard_map.46 = bf16[128,4096]{1,0:T(8,128)(2,1)} custom-call(s32[1,8,2]{2,1,0:T(8,128)} %copy.5.picks_hbm, bf16[128,4096]{1,0:T(8,128)(2,1)} %q_hbm.1, bf16[3,128,1024]{2,1,0:T(8,128)(2,1)} %k_hbm.1, bf16[3,128,1024]{2,1,0:T(8,128)(2,1)} %v_hbm.1), custom_call_target="tpu_custom_call" | custom-call | tf_op jit(solution)/shard_map/pallas_call | solution.py:402
  64.3 2.3 %copy.7 = bf16[128,4096]{1,0:T(8,128)(2,1)} copy(bf16[128,4096]{1,0:T(8,128)(2,1)} %shard_map.46) | data formatting | bytes 2097152

commit v4 on v3

--- a/solution.py
+++ b/solution.py
@@ -134,7 +134,8 @@
 
     column = y == core
     routes = [
-        (column & (z + 1 < depth), ((z + 1) * 2 + y) * 2 + core),
+        (column & (z == 0), (far * 2 + y) * 2 + core) for far in range(depth - 1, 0, -1)
+    ] + [
         (column & jnp.logical_not((core == 1) & (z == 0)), (z * 2 + 1 - y) * 2 + core),
         ((chip == 0) & (core == 1), 3),
     ]
@@ -191,7 +192,7 @@
         pk_copy(k).wait_recv()
         return carry
 
-    early = column & (chip != 0) & (z <= 1)
+    early = column & (chip != 0) & (z == 0)
 
     @pl.when(early)
     def _():
@@ -233,7 +234,7 @@
         return carry
 
     for ch in range(CHUNKS):
-        @pl.when(column & (chip != 0) & ((z > 1) | (ch >= 2)))
+        @pl.when(column & (chip != 0) & (z == 0) & (ch >= 2))
         def _():
             blk_copy(0, ch).wait_recv()
             blk_start(ch)
@@ -249,7 +250,7 @@
     fwd_copy(0).start()
     lax.fori_loop(0, KVH, load_queries, 0)
 
-    @pl.when(jnp.logical_not(column) & (chip != 0))
+    @pl.when((jnp.logical_not(column) | (z > 0)) & (chip != 0))
     def _():
         for ch in range(CHUNKS):
             blk_copy(0, ch).wait_recv()
@@ -424,7 +425,7 @@
                 pltpu.VMEM((half, width), bf16),
                 dma((2, KVH)), dma((KVH, GRP)), dma((2,)), dma((2,)), dma((2,)), dma((2,)),
                 dma((n,)), dma((n,)), dma((2,)),
-                dma((6, CHUNKS)), dma((2, CHUNKS)),
+                dma((n // 2 + 2, CHUNKS)), dma((2, CHUNKS)),
                 dma((n,)), dma((n,)), dma((n,)), dma((n,)), dma((KVH,)),
             ],
             compiler_params=pltpu.CompilerParams(

time: 66.9 us -> 67.8 us (1.013)
  the two profiles are of different devices: /device:TPU:25 before, /device:TPU:9 now
where the time goes in v4:
time: 67.8 us; the launch traced here: 67.5 us
  Pallas kernels  63.9 us (94%)
  local copies, waits for them, and re-layouts  3.63 us (5%)
    pallas_call x1, Pallas kernels, shard(): pl.pallas_call(functools.partial(kernel, n, slots), out_shape=jax.ShapeDt...  63.9 us
    unnamed x2, local copies, waits for them, and re-layouts  3.63 us

profile of v4, /device:TPU:9, one launch (start us, length us, event | category | flops | bytes accessed | tf_op | source)
XLA Modules:
  0.0 67.5 jit_solution(223715338533841659)
XLA Ops:
  0.0 1.3 %copy.5.picks_hbm = s32[1,8,2]{2,1,0:T(8,128)} copy(s32[1,8,2]{1,2,0:T(2,128)} %param.7) | data formatting | bytes 128 | tf_op args[3]
  1.3 63.9 %shard_map.46 = bf16[128,4096]{1,0:T(8,128)(2,1)} custom-call(s32[1,8,2]{2,1,0:T(8,128)} %copy.5.picks_hbm, bf16[128,4096]{1,0:T(8,128)(2,1)} %q_hbm.1, bf16[3,128,1024]{2,1,0:T(8,128)(2,1)} %k_hbm.1, bf16[3,128,1024]{2,1,0:T(8,128)(2,1)} %v_hbm.1), custom_call_target="tpu_custom_call" | custom-call | tf_op jit(solution)/shard_map/pallas_call | solution.py:403
  65.2 2.3 %copy.7 = bf16[128,4096]{1,0:T(8,128)(2,1)} copy(bf16[128,4096]{1,0:T(8,128)(2,1)} %shard_map.46) | data formatting | bytes 2097152
